TPU v7x, 32 devices: a whole 2x2x4 slice. The times are simulated.
32 devices in a mesh: gx: 8 (over z, x), gy: 4 (over y, core).
Axes of the slice: x: 2, y: 2, z: 4, core: 2. Of those that a mesh axis runs over, the one named last changes fastest.
Arguments:
- prediction: float32 [128, 64, 128], P('gx', 'gy'), may hold values from 0 to 1
- label_mask: int32 [128, 64, 128], P('gx', 'gy'), may hold values 0 or 1
- confidence: float32 [128, 64, 128], P('gx', 'gy'), may hold values from 0.5 to 1
Outputs:
- gradient: float32 [128, 64, 128], P('gx', 'gy')
- loss: float32 [], replicated
All inputs are finite; a program needn't handle non-finite values. No bound on the sum of `label_mask` on one device may be relied on, other than what follows from the above.
Results may differ from a plain program's by a relative error of at most 0.000025.
Values sent between devices are 32-bit elements; how exact they have to be, the bound alone decides.
A program may use at most 128 MiB of HBM per device.

v0:
```python
import functools

import jax
import jax.numpy as jnp
from jax import lax
from jax.experimental import pallas as pl
from jax.experimental.pallas import tpu as pltpu
from jax.sharding import PartitionSpec as P

ITERS = 3
STAGES = ITERS + 1
DEPTH = ITERS + 2
XO = 8
YE = 8
YW = 12
MESH = pl.DeviceIdType.MESH
XL, XU, YL, YU, ZL, ZU, CC = range(7)
LO, UP, MID = range(3)
DIRS = ((-1, 0), (1, 0), (0, -1), (0, 1), (-1, -1), (-1, 1), (1, -1), (1, 1))


def share(winner, other):
    return jnp.where(winner < other, 1.0, jnp.where(winner == other, 0.5, 0.0))


def loop(low, high, body, step=2):
    count = (high - low) // step

    @pl.loop(0, count)
    def _(index):
        for k in range(step):
            body(low + index * step + k)

    for row in range(low + count * step, high):
        body(row)


def kernel(
    sizes, pred_hbm, label_hbm, conf_hbm, out, loss,
    vol, lab, conf, skel, dels, befores, coefs, pool, wgt, wx, wy, wz, grad, hz, hy, final,
    part, slots_y, slots_x, got_x, got_y, got_c,
    in_sem, halo_send, halo_recv, sy_send, sy_recv, sx_send, sx_recv, g_send, g_recv,
):
    rows, cols, planes, ngx, ngy = sizes
    gx, gy = lax.axis_index("gx"), lax.axis_index("gy")
    own_x, own_y, own_w = pl.ds(XO, rows), pl.ds(YE, cols), pl.ds(YW, cols)
    span = cols + 8
    lanes = lax.broadcasted_iota(jnp.int32, (1, planes), 1)
    at_first, at_last = lanes == 0, lanes == planes - 1

    loads = [
        pltpu.make_async_copy(pred_hbm, vol.at[0, 0, own_x, own_y], in_sem.at[0]),
        pltpu.make_async_copy(label_hbm, lab, in_sem.at[1]),
        pltpu.make_async_copy(conf_hbm, conf, in_sem.at[2]),
    ]
    for copy in loads:
        copy.start()

    def there(dx, dy):
        found = None
        for d, me, size in ((dx, gx, ngx), (dy, gy, ngy)):
            if d:
                inside = (me > 0) if d < 0 else (me < size - 1)
                found = inside if found is None else jnp.logical_and(found, inside)
        return found

    barrier = pltpu.get_barrier_semaphore()
    for k in range(1, ngx):
        pl.semaphore_signal(barrier, inc=1, device_id=(lax.rem(gx + k, ngx), gy), device_id_type=MESH)
    for k in range(1, ngy):
        pl.semaphore_signal(barrier, inc=1, device_id=(gx, lax.rem(gy + k, ngy)), device_id_type=MESH)
    for dx, dy in DIRS[4:]:
        @pl.when(there(dx, dy))
        def _(dx=dx, dy=dy):
            pl.semaphore_signal(barrier, inc=1, device_id=(gx + dx, gy + dy), device_id_type=MESH)

    for copy in loads:
        copy.wait()

    def make_target(row):
        vol[0, 1, XO + row, YE : YE + cols] = lab[row].astype(jnp.float32) * conf[row]

    loop(0, rows, make_target)

    corners = 1
    for me, size in ((gx, ngx), (gy, ngy)):
        corners *= lax.div(me + size - 1, size) + lax.div(2 * size - 2 - me, size)
    pl.semaphore_wait(barrier, ngx - 1 + ngy - 1 + corners)

    def strip(d, length, offset, width, outside):
        if d == 0:
            return pl.ds(offset, length)
        if d < 0:
            return pl.ds(offset - width if outside else offset, width)
        return pl.ds(offset + length if outside else offset + length - width, width)

    halos = []
    for k, (dx, dy) in enumerate(DIRS):
        copy = pltpu.make_async_remote_copy(
            src_ref=vol.at[0, :, strip(dx, rows, XO, DEPTH, False), strip(dy, cols, YE, 8, False)],
            dst_ref=vol.at[0, :, strip(-dx, rows, XO, DEPTH, True), strip(-dy, cols, YE, 8, True)],
            send_sem=halo_send.at[k],
            recv_sem=halo_recv.at[k],
            device_id=(gx + dx, gy + dy),
            device_id_type=MESH,
        )
        halos.append(copy)
        pl.when(there(dx, dy))(copy.start)

    def clear_grad(row):
        for i in range(STAGES + 1):
            grad[i, row] = jnp.zeros((cols + 24, planes), jnp.float32)

    loop(XO - DEPTH - 1, XO + rows + DEPTH + 1, clear_grad)
    for i in range(STAGES):
        reach = STAGES - i
        for row in (XO - reach - 2, XO - reach - 1, XO + rows + reach, XO + rows + reach + 1):
            for kind in range(7):
                wgt[i, kind, row] = jnp.zeros((cols + 24, planes), jnp.float32)
        for row in (XO - 2, XO - 1, XO + rows, XO + rows + 1):
            hy[i, row] = jnp.zeros((span, planes), jnp.float32)
            for kind in range(3):
                wx[i, kind, row] = jnp.zeros((span, planes), jnp.float32)

    tile = jnp.zeros((8, planes), jnp.float32)

    def clear_sides(row):
        for i in range(STAGES):
            for kind in range(7):
                if i == 0 or kind == YU:
                    wgt[i, kind, row, 0:8] = tile
                if i == 0 or kind == YL:
                    wgt[i, kind, row, cols + 16 : cols + 24] = tile

    loop(XO - STAGES, XO + rows + STAGES, clear_sides)

    def clear_pools(row):
        for i in range(STAGES):
            hz[i, row, YW - 8 : YW] = tile
            hz[i, row, YW + cols : YW + cols + 8] = tile
            for kind in range(3):
                wy[i, kind, row, YW - 8 : YW] = tile
                wy[i, kind, row, YW + cols : YW + cols + 8] = tile

    loop(0, rows, clear_pools)

    for k, (dx, dy) in enumerate(DIRS):
        pl.when(there(-dx, -dy))(halos[k].wait_recv)

    def stand_in(i):
        reach = DEPTH - i
        every = pl.ds(XO - reach, rows + 2 * reach)

        @pl.when(gy == 0)
        def _():
            vol[i, :, every, YE - 1 : YE] = vol[i, :, every, YE : YE + 1]

        @pl.when(gy == ngy - 1)
        def _():
            vol[i, :, every, YE + cols : YE + cols + 1] = vol[i, :, every, YE + cols - 1 : YE + cols]

        @pl.when(gx == 0)
        def _():
            vol[i, :, XO - 1] = vol[i, :, XO]

        @pl.when(gx == ngx - 1)
        def _():
            vol[i, :, XO + rows] = vol[i, :, XO + rows - 1]

    def before(value, edge):
        return jnp.where(at_first, edge, pltpu.roll(value, 1, 1))

    def after(value):
        return jnp.where(at_last, value, pltpu.roll(value, planes - 1, 1))

    def erode_step(i):
        reach = STAGES - i

        def step(row):
            for v in range(2):
                mid = vol[i, v, row, 4 : 4 + span]
                least = jnp.minimum(vol[i, v, row - 1, 4 : 4 + span], vol[i, v, row + 1, 4 : 4 + span])
                sides = jnp.minimum(vol[i, v, row, 3 : 3 + span], vol[i, v, row, 5 : 5 + span])
                along = jnp.minimum(before(mid, mid), after(mid))
                vol[i + 1, v, row, 4 : 4 + span] = jnp.minimum(jnp.minimum(least, sides), jnp.minimum(along, mid))

        loop(XO - reach, XO + rows + reach, step)
        stand_in(i + 1)

    def delta_step(i):
        def step(row):
            for v in range(2):
                most = None
                for x in (-1, 0, 1):
                    for y in (-1, 0, 1):
                        value = vol[i + 1, v, XO + row + x, YE + y : YE + y + cols]
                        most = value if most is None else jnp.maximum(most, value)
                most = jnp.maximum(jnp.maximum(before(most, most), most), after(most))
                delta = jnp.maximum(vol[i, v, XO + row, YE : YE + cols] - most, 0.0)
                if i == 0:
                    result = delta
                else:
                    old = skel[v, row]
                    result = old + jnp.maximum(delta - old * delta, 0.0)
                skel[v, row] = result
                if v == 0:
                    dels[i, row] = delta
                    if i > 0:
                        befores[i, row] = old

        loop(0, rows, step)

    stand_in(0)
    for i in range(STAGES):
        erode_step(i)
        delta_step(i)

    def add_up(row, sums):
        sum_a, sum_b, sum_c, sum_d = sums
        skel_pred, skel_target = skel[0, row], skel[1, row]
        return (
            sum_a + skel_pred * vol[0, 1, XO + row, YE : YE + cols],
            sum_b + skel_pred,
            sum_c + skel_target * vol[0, 0, XO + row, YE : YE + cols],
            sum_d + skel_target,
        )

    sums = lax.fori_loop(0, rows, add_up, (jnp.zeros((cols, planes), jnp.float32),) * 4)
    part[...] = jnp.zeros_like(part)
    for k in range(4):
        part[k : k + 1] = jnp.sum(sums[k], axis=0, keepdims=True)

    slots_y[gy] = part[...]
    copies_y = []
    for k in range(1, ngy):
        copy = pltpu.make_async_remote_copy(
            src_ref=part, dst_ref=slots_y.at[gy], send_sem=sy_send.at[k], recv_sem=sy_recv.at[k],
            device_id=(gx, lax.rem(gy + k, ngy)), device_id_type=MESH,
        )
        copy.start()
        copies_y.append(copy)

    def split(total, low, mid, high, first, sign):
        to_high = share(high, first) if sign > 0 else share(first, high)
        to_low = share(low, mid) if sign > 0 else share(mid, low)
        high_part = total * to_high
        rest = total - high_part
        low_part = rest * to_low
        return low_part, high_part, rest - low_part

    def dilate_weights(row):
        for i in range(STAGES):
            low, mid, high = [vol[i + 1, 0, XO + row + x, 4 : 4 + span] for x in (-1, 0, 1)]
            first = jnp.maximum(low, mid)
            to_low, to_high, to_mid = split(1.0, low, mid, high, first, -1)
            wx[i, LO, XO + row] = to_low
            wx[i, UP, XO + row] = to_high
            wx[i, MID, XO + row] = to_mid
            pool[i, row] = jnp.maximum(first, high)

    loop(0, rows, dilate_weights, 1)

    def dilate_weights_2(row):
        below = 1.0
        for i in reversed(range(STAGES)):
            low, mid, high = [pool[i, row, 4 + y : 4 + y + cols] for y in (-1, 0, 1)]
            first = jnp.maximum(low, mid)
            to_low, to_high, to_mid = split(1.0, low, mid, high, first, -1)
            wy[i, LO, row, YW : YW + cols] = to_low
            wy[i, UP, row, YW : YW + cols] = to_high
            wy[i, MID, row, YW : YW + cols] = to_mid
            mid = jnp.maximum(first, high)
            low, high = before(mid, -jnp.inf), after(mid)
            first = jnp.maximum(low, mid)
            to_low, to_high, to_mid = split(1.0, low, mid, high, first, -1)
            wz[i, LO, row] = to_low
            wz[i, UP, row] = jnp.where(at_last, 0.0, to_high)
            wz[i, MID, row] = jnp.where(at_last, to_high + to_mid, to_mid)
            delta = dels[i, row]
            if i > 0:
                old = befores[i, row]
                passed = jnp.where(delta - old * delta > 0.0, below, 0.0)
                coefs[i, row] = passed - passed * old
                below = below - passed * delta
            else:
                coefs[i, row] = jnp.where(delta > 0.0, below, 0.0)

    loop(0, rows, dilate_weights_2, 1)

    @pl.when(gy == 0)
    def _():
        edge = pl.ds(YW, 1)
        for i in range(STAGES):
            wy[i, MID, :, edge] = wy[i, MID, :, edge] + wy[i, LO, :, edge]
            wy[i, LO, :, edge] = jnp.zeros((rows, 1, planes), jnp.float32)

    @pl.when(gy == ngy - 1)
    def _():
        edge = pl.ds(YW + cols - 1, 1)
        for i in range(STAGES):
            wy[i, MID, :, edge] = wy[i, MID, :, edge] + wy[i, UP, :, edge]
            wy[i, UP, :, edge] = jnp.zeros((rows, 1, planes), jnp.float32)

    @pl.when(gx == 0)
    def _():
        for i in range(STAGES):
            wx[i, MID, XO] = wx[i, MID, XO] + wx[i, LO, XO]
            wx[i, LO, XO] = jnp.zeros((span, planes), jnp.float32)

    @pl.when(gx == ngx - 1)
    def _():
        edge = XO + rows - 1
        for i in range(STAGES):
            wx[i, MID, edge] = wx[i, MID, edge] + wx[i, UP, edge]
            wx[i, UP, edge] = jnp.zeros((span, planes), jnp.float32)

    def erode_weights(i):
        reach = STAGES - i
        every = pl.ds(XO - reach, rows + 2 * reach)
        mine = slice(8, 8 + span)

        def step(row):
            mid = vol[i, 0, row, 4 : 4 + span]
            x_low, x_high = vol[i, 0, row - 1, 4 : 4 + span], vol[i, 0, row + 1, 4 : 4 + span]
            y_low, y_high = vol[i, 0, row, 3 : 3 + span], vol[i, 0, row, 5 : 5 + span]
            z_low, z_high = before(mid, jnp.inf), after(mid)
            x_first, y_first, z_first = [jnp.minimum(low, mid) for low in (x_low, y_low, z_low)]
            x_pool, y_pool = jnp.minimum(x_first, x_high), jnp.minimum(y_first, y_high)
            z_pool = jnp.minimum(z_first, z_high)
            to_z = share(z_pool, jnp.minimum(x_pool, y_pool))
            rest = 1.0 - to_z
            to_y = rest * share(y_pool, x_pool)
            x_parts = split(rest - to_y, x_low, mid, x_high, x_first, 1)
            y_parts = split(to_y, y_low, mid, y_high, y_first, 1)
            z_parts = split(to_z, z_low, mid, z_high, z_first, 1)
            wgt[i, XL, row, mine] = x_parts[0]
            wgt[i, XU, row, mine] = x_parts[1]
            wgt[i, YL, row, mine] = y_parts[0]
            wgt[i, YU, row, mine] = y_parts[1]
            wgt[i, ZL, row, mine] = z_parts[0]
            wgt[i, ZU, row, mine] = jnp.where(at_last, 0.0, z_parts[1])
            centre = x_parts[2] + y_parts[2] + z_parts[2]
            wgt[i, CC, row, mine] = jnp.where(at_last, centre + z_parts[1], centre)

        loop(XO - reach, XO + rows + reach, step)

        for there_is_none, edge, kind in ((gy == 0, YW, YL), (gy == ngy - 1, YW + cols - 1, YU)):
            @pl.when(there_is_none)
            def _(edge=pl.ds(edge, 1), kind=kind):
                wgt[i, CC, every, edge] = wgt[i, CC, every, edge] + wgt[i, kind, every, edge]
                wgt[i, kind, every, edge] = jnp.zeros((rows + 2 * reach, 1, planes), jnp.float32)

        for there_is_none, edge, kind in ((gx == 0, XO, XL), (gx == ngx - 1, XO + rows - 1, XU)):
            @pl.when(there_is_none)
            def _(edge=edge, kind=kind):
                wgt[i, CC, edge, mine] = wgt[i, CC, edge, mine] + wgt[i, kind, edge, mine]
                wgt[i, kind, edge, mine] = jnp.zeros((span, planes), jnp.float32)

    erode_weights(0)

    for copy in copies_y:
        copy.wait()
    total = slots_y[0]
    for k in range(1, ngy):
        total = total + slots_y[k]
    part[...] = total
    slots_x[gx] = total
    copies_x = []
    for k in range(1, ngx):
        copy = pltpu.make_async_remote_copy(
            src_ref=part, dst_ref=slots_x.at[gx], send_sem=sx_send.at[k], recv_sem=sx_recv.at[k],
            device_id=(lax.rem(gx + k, ngx), gy), device_id_type=MESH,
        )
        copy.start()
        copies_x.append(copy)

    for i in range(1, STAGES):
        erode_weights(i)

    for copy in copies_x:
        copy.wait()
    total = slots_x[0]
    for k in range(1, ngx):
        total = total + slots_x[k]
    sum_a, sum_b, sum_c, sum_d = [jnp.sum(total[k : k + 1], axis=1, keepdims=True) for k in range(4)]
    precision = (sum_a + 1.0) / (sum_b + 1.0)
    sensitivity = (sum_c + 1.0) / (sum_d + 1.0)
    together = precision + sensitivity
    loss[...] = 1.0 - 2.0 * precision * sensitivity / together
    cells = float(rows * ngx * cols * ngy * planes)
    coef_pred = cells * (-2.0 * sensitivity * sensitivity / (together * together)) / (sum_b + 1.0)
    coef_target = cells * (-2.0 * precision * precision / (together * together)) / (sum_d + 1.0)
    precision, coef_pred, coef_target = [
        jnp.broadcast_to(value, (cols, planes)) for value in (precision, coef_pred, coef_target)
    ]

    def start_back(row):
        cotangent = coef_pred * (vol[0, 1, XO + row, YE : YE + cols] - precision)
        for i in range(STAGES):
            given = cotangent * coefs[i, row]
            grad[i, XO + row, YW : YW + cols] = given
            hz[i, row, YW : YW + cols] = -(
                given * wz[i, MID, row]
                + pltpu.roll(given * wz[i, LO, row], planes - 1, 1)
                + pltpu.roll(given * wz[i, UP, row], 1, 1)
            )

    loop(0, rows, start_back, 1)

    def back_columns(row):
        for i in range(STAGES):
            hy[i, XO + row] = (
                wy[i, MID, row, 8 : 8 + span] * hz[i, row, 8 : 8 + span]
                + wy[i, LO, row, 9 : 9 + span] * hz[i, row, 9 : 9 + span]
                + wy[i, UP, row, 7 : 7 + span] * hz[i, row, 7 : 7 + span]
            )

    loop(0, rows, back_columns, 1)

    def back_rows(row):
        for i in range(STAGES):
            grad[i + 1, row, 8 : 8 + span] = grad[i + 1, row, 8 : 8 + span] + (
                wx[i, MID, row] * hy[i, row]
                + wx[i, LO, row + 1] * hy[i, row + 1]
                + wx[i, UP, row - 1] * hy[i, row - 1]
            )

    loop(XO - 1, XO + rows + 1, back_rows, 1)

    def gather(i, row, low, length):
        here = slice(low, low + length)
        up, down = slice(low + 1, low + 1 + length), slice(low - 1, low - 1 + length)
        value = grad[i + 1, row, here]
        return (
            grad[i, row, here]
            + wgt[i, CC, row, here] * value
            + wgt[i, XL, row + 1, here] * grad[i + 1, row + 1, here]
            + wgt[i, XU, row - 1, here] * grad[i + 1, row - 1, here]
            + wgt[i, YL, row, up] * grad[i + 1, row, up]
            + wgt[i, YU, row, down] * grad[i + 1, row, down]
            + pltpu.roll(wgt[i, ZL, row, here] * value, planes - 1, 1)
            + pltpu.roll(wgt[i, ZU, row, here] * value, 1, 1)
        )

    for i in reversed(range(1, STAGES)):
        def step(row, i=i):
            grad[i, row, 8 : 8 + span] = gather(i, row, 8, span)

        loop(XO - DEPTH + i, XO + rows + DEPTH - i, step)

    def last_step(row):
        final[row] = gather(0, row, YW - 8, cols + 16)

    loop(XO - DEPTH, XO + rows + DEPTH, last_step)

    returns = []
    for k, (dx, dy) in enumerate(DIRS):
        if dx and dy:
            place = got_c.at[k - 4]
        elif dx:
            place = got_x.at[k]
        else:
            place = got_y.at[k - 2]
        copy = pltpu.make_async_remote_copy(
            src_ref=final.at[strip(dx, rows, XO, DEPTH, True), strip(dy, cols, YE, 8, True)],
            dst_ref=place,
            send_sem=g_send.at[k],
            recv_sem=g_recv.at[k],
            device_id=(gx + dx, gy + dy),
            device_id_type=MESH,
        )
        returns.append((copy, place))
        pl.when(there(dx, dy))(copy.start)

    def finish(row):
        out[row] = final[XO + row, YE : YE + cols] + coef_target * skel[1, row]

    loop(0, rows, finish)

    for k, (dx, dy) in enumerate(DIRS):
        copy, place = returns[k]

        @pl.when(there(-dx, -dy))
        def _(copy=copy, place=place, dx=dx, dy=dy):
            copy.wait_recv()
            at = (strip(-dx, rows, 0, DEPTH, False), strip(-dy, cols, 0, 8, False))
            out[at] = out[at] + place[...]

    for k, (dx, dy) in enumerate(DIRS):
        @pl.when(there(dx, dy))
        def _(k=k):
            halos[k].wait_send()
            returns[k][0].wait_send()


def body(prediction, label_mask, confidence):
    rows, cols, planes = prediction.shape
    ngx, ngy = lax.axis_size("gx"), lax.axis_size("gy")
    f32 = jnp.float32
    wide = rows + 2 * XO
    dma = pltpu.SemaphoreType.DMA
    gradient, loss = pl.pallas_call(
        functools.partial(kernel, (rows, cols, planes, ngx, ngy)),
        out_shape=(jax.ShapeDtypeStruct((rows, cols, planes), f32), jax.ShapeDtypeStruct((1, 1), f32)),
        in_specs=[pl.BlockSpec(memory_space=pl.ANY)] * 3,
        out_specs=(pl.BlockSpec(memory_space=pltpu.VMEM), pl.BlockSpec(memory_space=pltpu.VMEM)),
        scratch_shapes=[
            pltpu.VMEM((STAGES + 1, 2, wide, cols + 16, planes), f32),
            pltpu.VMEM((rows, cols, planes), jnp.int32),
            pltpu.VMEM((rows, cols, planes), f32),
            pltpu.VMEM((2, rows, cols, planes), f32),
            pltpu.VMEM((STAGES, rows, cols, planes), f32),
            pltpu.VMEM((STAGES, rows, cols, planes), f32),
            pltpu.VMEM((STAGES, rows, cols, planes), f32),
            pltpu.VMEM((STAGES, rows, cols + 8, planes), f32),
            pltpu.VMEM((STAGES, 7, wide, cols + 24, planes), f32),
            pltpu.VMEM((STAGES, 3, wide, cols + 8, planes), f32),
            pltpu.VMEM((STAGES, 3, rows, cols + 24, planes), f32),
            pltpu.VMEM((STAGES, 3, rows, cols, planes), f32),
            pltpu.VMEM((STAGES + 1, wide, cols + 24, planes), f32),
            pltpu.VMEM((STAGES, rows, cols + 24, planes), f32),
            pltpu.VMEM((STAGES, wide, cols + 8, planes), f32),
            pltpu.VMEM((wide, cols + 16, planes), f32),
            pltpu.VMEM((8, planes), f32),
            pltpu.VMEM((ngy, 8, planes), f32),
            pltpu.VMEM((ngx, 8, planes), f32),
            pltpu.VMEM((2, DEPTH, cols, planes), f32),
            pltpu.VMEM((2, rows, 8, planes), f32),
            pltpu.VMEM((4, DEPTH, 8, planes), f32),
            dma((3,)),
            dma((8,)),
            dma((8,)),
            dma((ngy,)),
            dma((ngy,)),
            dma((ngx,)),
            dma((ngx,)),
            dma((8,)),
            dma((8,)),
        ],
        compiler_params=pltpu.CompilerParams(
            collective_id=0, has_side_effects=True, vmem_limit_bytes=60 * 1024 * 1024
        ),
    )(prediction, label_mask, confidence)
    return gradient, loss[0, 0]


def solution(mesh):
    placed = (P("gx", "gy", None), P("gx", "gy", None), P("gx", "gy", None))
    return jax.shard_map(
        body, mesh=mesh, in_specs=placed, out_specs=(P("gx", "gy", None), P()), check_vma=False
    )
```

profile of v0, /device:TPU:0, one launch (start us, length us, event | category | flops | bytes accessed | tf_op | source)
XLA Modules:
  0.0 42.6 jit_solution(5643839631340541868)
XLA Ops:
  0.6 38.6 %shard_map.50 = (f32[16,16,128]{2,1,0:T(8,128)}, f32[1,1]{1,0:T(1,128)}) custom-call(f32[16,16,128]{2,1,0:T(8,128)} %pred_hbm.1, s32[16,16,128]{2,1,0:T(8,128)} %label_hbm.1, f32[16,16,128]{2,1,0:T(8,128)} %conf_hbm.1), custom_call_target="tpu_custom_call" | custom-call | tf_op jit(solution)/shard_map/pallas_call | solution.py:502
  39.2 1.6 %copy.7 = f32[16,16,128]{2,1,0:T(8,128)} copy(f32[16,16,128]{2,1,0:T(8,128)} %get-tuple-element.8) | data formatting | bytes 262144
where the time goes:
time: 43.2 us; the launch traced here: 42.6 us
  Pallas kernels  38.6 us (89%)
  between operations  2.45 us (6%)
  local copies, waits for them, and re-layouts  1.57 us (4%)
    pallas_call x1, Pallas kernels, body(): pl.pallas_call(functools.partial(kernel, (rows, cols, planes, ngx, ngy)),...  38.6 us
    unnamed x1, local copies, waits for them, and re-layouts  1.57 us

commit v1 on v0

--- a/solution.py
+++ b/solution.py
@@ -23,21 +23,39 @@
     return jnp.where(winner < other, 1.0, jnp.where(winner == other, 0.5, 0.0))
 
 
-def loop(low, high, body, step=2):
+def loop(low, high, body, step=4):
     count = (high - low) // step
 
-    @pl.loop(0, count)
-    def _(index):
-        for k in range(step):
-            body(low + index * step + k)
+    if count == 1:
+        for row in range(low, low + step):
+            body(row)
+    else:
+
+        @pl.loop(0, count)
+        def _(index):
+            for k in range(step):
+                body(low + index * step + k)
 
     for row in range(low + count * step, high):
         body(row)
 
 
+def halves(*parts):
+    @pl.loop(0, 2)
+    def _(index):
+        for low, high, body in parts:
+            step = (high - low) // 2
+            for k in range(step):
+                body(low + index * step + k)
+
+    for low, high, body in parts:
+        if (high - low) % 2:
+            body(high - 1)
+
+
 def kernel(
     sizes, pred_hbm, label_hbm, conf_hbm, out, loss,
-    vol, lab, conf, skel, dels, befores, coefs, pool, wgt, wx, wy, wz, grad, hz, hy, final,
+    vol, lab, conf, skel, dels, coefs, pool, wgt, wx, wy, wz, base, grad, hz, hy, final,
     part, slots_y, slots_x, got_x, got_y, got_c,
     in_sem, halo_send, halo_recv, sy_send, sy_recv, sx_send, sx_recv, g_send, g_recv,
 ):
@@ -49,7 +67,7 @@
     at_first, at_last = lanes == 0, lanes == planes - 1
 
     loads = [
-        pltpu.make_async_copy(pred_hbm, vol.at[0, 0, own_x, own_y], in_sem.at[0]),
+        pltpu.make_async_copy(pred_hbm, vol[0].at[0, own_x, own_y], in_sem.at[0]),
         pltpu.make_async_copy(label_hbm, lab, in_sem.at[1]),
         pltpu.make_async_copy(conf_hbm, conf, in_sem.at[2]),
     ]
@@ -78,7 +96,7 @@
         copy.wait()
 
     def make_target(row):
-        vol[0, 1, XO + row, YE : YE + cols] = lab[row].astype(jnp.float32) * conf[row]
+        vol[0][1, XO + row, YE : YE + cols] = lab[row].astype(jnp.float32) * conf[row]
 
     loop(0, rows, make_target)
 
@@ -97,8 +115,8 @@
     halos = []
     for k, (dx, dy) in enumerate(DIRS):
         copy = pltpu.make_async_remote_copy(
-            src_ref=vol.at[0, :, strip(dx, rows, XO, DEPTH, False), strip(dy, cols, YE, 8, False)],
-            dst_ref=vol.at[0, :, strip(-dx, rows, XO, DEPTH, True), strip(-dy, cols, YE, 8, True)],
+            src_ref=vol[0].at[:, strip(dx, rows, XO, DEPTH, False), strip(dy, cols, YE, 8, False)],
+            dst_ref=vol[0].at[:, strip(-dx, rows, XO, DEPTH, True), strip(-dy, cols, YE, 8, True)],
             send_sem=halo_send.at[k],
             recv_sem=halo_recv.at[k],
             device_id=(gx + dx, gy + dy),
@@ -109,7 +127,9 @@
 
     def clear_grad(row):
         for i in range(STAGES + 1):
-            grad[i, row] = jnp.zeros((cols + 24, planes), jnp.float32)
+            base[i][row] = jnp.zeros((cols + 24, planes), jnp.float32)
+            if 0 < i < STAGES:
+                grad[i][row] = jnp.zeros((cols + 24, planes), jnp.float32)
 
     loop(XO - DEPTH - 1, XO + rows + DEPTH + 1, clear_grad)
     for i in range(STAGES):
@@ -153,19 +173,19 @@
 
         @pl.when(gy == 0)
         def _():
-            vol[i, :, every, YE - 1 : YE] = vol[i, :, every, YE : YE + 1]
+            vol[i][:, every, YE - 1 : YE] = vol[i][:, every, YE : YE + 1]
 
         @pl.when(gy == ngy - 1)
         def _():
-            vol[i, :, every, YE + cols : YE + cols + 1] = vol[i, :, every, YE + cols - 1 : YE + cols]
+            vol[i][:, every, YE + cols : YE + cols + 1] = vol[i][:, every, YE + cols - 1 : YE + cols]
 
         @pl.when(gx == 0)
         def _():
-            vol[i, :, XO - 1] = vol[i, :, XO]
+            vol[i][:, XO - 1] = vol[i][:, XO]
 
         @pl.when(gx == ngx - 1)
         def _():
-            vol[i, :, XO + rows] = vol[i, :, XO + rows - 1]
+            vol[i][:, XO + rows] = vol[i][:, XO + rows - 1]
 
     def before(value, edge):
         return jnp.where(at_first, edge, pltpu.roll(value, 1, 1))
@@ -178,14 +198,13 @@
 
         def step(row):
             for v in range(2):
-                mid = vol[i, v, row, 4 : 4 + span]
-                least = jnp.minimum(vol[i, v, row - 1, 4 : 4 + span], vol[i, v, row + 1, 4 : 4 + span])
-                sides = jnp.minimum(vol[i, v, row, 3 : 3 + span], vol[i, v, row, 5 : 5 + span])
+                mid = vol[i][v, row, 4 : 4 + span]
+                least = jnp.minimum(vol[i][v, row - 1, 4 : 4 + span], vol[i][v, row + 1, 4 : 4 + span])
+                sides = jnp.minimum(vol[i][v, row, 3 : 3 + span], vol[i][v, row, 5 : 5 + span])
                 along = jnp.minimum(before(mid, mid), after(mid))
-                vol[i + 1, v, row, 4 : 4 + span] = jnp.minimum(jnp.minimum(least, sides), jnp.minimum(along, mid))
-
-        loop(XO - reach, XO + rows + reach, step)
-        stand_in(i + 1)
+                vol[i + 1][v, row, 4 : 4 + span] = jnp.minimum(jnp.minimum(least, sides), jnp.minimum(along, mid))
+
+        return XO - reach, XO + rows + reach, step
 
     def delta_step(i):
         def step(row):
@@ -193,39 +212,42 @@
                 most = None
                 for x in (-1, 0, 1):
                     for y in (-1, 0, 1):
-                        value = vol[i + 1, v, XO + row + x, YE + y : YE + y + cols]
+                        value = vol[i + 1][v, XO + row + x, YE + y : YE + y + cols]
                         most = value if most is None else jnp.maximum(most, value)
                 most = jnp.maximum(jnp.maximum(before(most, most), most), after(most))
-                delta = jnp.maximum(vol[i, v, XO + row, YE : YE + cols] - most, 0.0)
+                delta = jnp.maximum(vol[i][v, XO + row, YE : YE + cols] - most, 0.0)
                 if i == 0:
                     result = delta
                 else:
-                    old = skel[v, row]
+                    old = skel[i - 1][v, row]
                     result = old + jnp.maximum(delta - old * delta, 0.0)
-                skel[v, row] = result
+                skel[i][v, row] = result
                 if v == 0:
                     dels[i, row] = delta
-                    if i > 0:
-                        befores[i, row] = old
-
-        loop(0, rows, step)
+
+        return 0, rows, step
 
     stand_in(0)
-    for i in range(STAGES):
-        erode_step(i)
-        delta_step(i)
+    halves(erode_step(0))
+    stand_in(1)
+    for i in range(1, STAGES):
+        halves(delta_step(i - 1), erode_step(i))
+        stand_in(i + 1)
+    halves(delta_step(STAGES - 1))
 
     def add_up(row, sums):
         sum_a, sum_b, sum_c, sum_d = sums
-        skel_pred, skel_target = skel[0, row], skel[1, row]
+        skel_pred, skel_target = skel[ITERS][0, row], skel[ITERS][1, row]
         return (
-            sum_a + skel_pred * vol[0, 1, XO + row, YE : YE + cols],
+            sum_a + skel_pred * vol[0][1, XO + row, YE : YE + cols],
             sum_b + skel_pred,
-            sum_c + skel_target * vol[0, 0, XO + row, YE : YE + cols],
+            sum_c + skel_target * vol[0][0, XO + row, YE : YE + cols],
             sum_d + skel_target,
         )
 
-    sums = lax.fori_loop(0, rows, add_up, (jnp.zeros((cols, planes), jnp.float32),) * 4)
+    sums = (jnp.zeros((cols, planes), jnp.float32),) * 4
+    for row in range(rows):
+        sums = add_up(row, sums)
     part[...] = jnp.zeros_like(part)
     for k in range(4):
         part[k : k + 1] = jnp.sum(sums[k], axis=0, keepdims=True)
@@ -250,7 +272,7 @@
 
     def dilate_weights(row):
         for i in range(STAGES):
-            low, mid, high = [vol[i + 1, 0, XO + row + x, 4 : 4 + span] for x in (-1, 0, 1)]
+            low, mid, high = [vol[i + 1][0, XO + row + x, 4 : 4 + span] for x in (-1, 0, 1)]
             first = jnp.maximum(low, mid)
             to_low, to_high, to_mid = split(1.0, low, mid, high, first, -1)
             wx[i, LO, XO + row] = to_low
@@ -258,7 +280,7 @@
             wx[i, MID, XO + row] = to_mid
             pool[i, row] = jnp.maximum(first, high)
 
-    loop(0, rows, dilate_weights, 1)
+    loop(0, rows, dilate_weights, 2)
 
     def dilate_weights_2(row):
         below = 1.0
@@ -278,14 +300,14 @@
             wz[i, MID, row] = jnp.where(at_last, to_high + to_mid, to_mid)
             delta = dels[i, row]
             if i > 0:
-                old = befores[i, row]
+                old = skel[i - 1][0, row]
                 passed = jnp.where(delta - old * delta > 0.0, below, 0.0)
                 coefs[i, row] = passed - passed * old
                 below = below - passed * delta
             else:
                 coefs[i, row] = jnp.where(delta > 0.0, below, 0.0)
 
-    loop(0, rows, dilate_weights_2, 1)
+    loop(0, rows, dilate_weights_2, 2)
 
     @pl.when(gy == 0)
     def _():
@@ -320,9 +342,9 @@
         mine = slice(8, 8 + span)
 
         def step(row):
-            mid = vol[i, 0, row, 4 : 4 + span]
-            x_low, x_high = vol[i, 0, row - 1, 4 : 4 + span], vol[i, 0, row + 1, 4 : 4 + span]
-            y_low, y_high = vol[i, 0, row, 3 : 3 + span], vol[i, 0, row, 5 : 5 + span]
+            mid = vol[i][0, row, 4 : 4 + span]
+            x_low, x_high = vol[i][0, row - 1, 4 : 4 + span], vol[i][0, row + 1, 4 : 4 + span]
+            y_low, y_high = vol[i][0, row, 3 : 3 + span], vol[i][0, row, 5 : 5 + span]
             z_low, z_high = before(mid, jnp.inf), after(mid)
             x_first, y_first, z_first = [jnp.minimum(low, mid) for low in (x_low, y_low, z_low)]
             x_pool, y_pool = jnp.minimum(x_first, x_high), jnp.minimum(y_first, y_high)
@@ -395,17 +417,17 @@
     ]
 
     def start_back(row):
-        cotangent = coef_pred * (vol[0, 1, XO + row, YE : YE + cols] - precision)
+        cotangent = coef_pred * (vol[0][1, XO + row, YE : YE + cols] - precision)
         for i in range(STAGES):
             given = cotangent * coefs[i, row]
-            grad[i, XO + row, YW : YW + cols] = given
+            base[i][XO + row, YW : YW + cols] = given
             hz[i, row, YW : YW + cols] = -(
                 given * wz[i, MID, row]
                 + pltpu.roll(given * wz[i, LO, row], planes - 1, 1)
                 + pltpu.roll(given * wz[i, UP, row], 1, 1)
             )
 
-    loop(0, rows, start_back, 1)
+    loop(0, rows, start_back, 4)
 
     def back_columns(row):
         for i in range(STAGES):
@@ -415,43 +437,44 @@
                 + wy[i, UP, row, 7 : 7 + span] * hz[i, row, 7 : 7 + span]
             )
 
-    loop(0, rows, back_columns, 1)
+    loop(0, rows, back_columns, 4)
 
     def back_rows(row):
         for i in range(STAGES):
-            grad[i + 1, row, 8 : 8 + span] = grad[i + 1, row, 8 : 8 + span] + (
+            base[i + 1][row, 8 : 8 + span] = base[i + 1][row, 8 : 8 + span] + (
                 wx[i, MID, row] * hy[i, row]
                 + wx[i, LO, row + 1] * hy[i, row + 1]
                 + wx[i, UP, row - 1] * hy[i, row - 1]
             )
 
-    loop(XO - 1, XO + rows + 1, back_rows, 1)
+    halves((XO - 1, XO + rows + 1, back_rows))
 
     def gather(i, row, low, length):
+        source = grad[i + 1] if i + 1 < STAGES else base[i + 1]
         here = slice(low, low + length)
         up, down = slice(low + 1, low + 1 + length), slice(low - 1, low - 1 + length)
-        value = grad[i + 1, row, here]
+        value = source[row, here]
         return (
-            grad[i, row, here]
+            base[i][row, here]
             + wgt[i, CC, row, here] * value
-            + wgt[i, XL, row + 1, here] * grad[i + 1, row + 1, here]
-            + wgt[i, XU, row - 1, here] * grad[i + 1, row - 1, here]
-            + wgt[i, YL, row, up] * grad[i + 1, row, up]
-            + wgt[i, YU, row, down] * grad[i + 1, row, down]
+            + wgt[i, XL, row + 1, here] * source[row + 1, here]
+            + wgt[i, XU, row - 1, here] * source[row - 1, here]
+            + wgt[i, YL, row, up] * source[row, up]
+            + wgt[i, YU, row, down] * source[row, down]
             + pltpu.roll(wgt[i, ZL, row, here] * value, planes - 1, 1)
             + pltpu.roll(wgt[i, ZU, row, here] * value, 1, 1)
         )
 
     for i in reversed(range(1, STAGES)):
         def step(row, i=i):
-            grad[i, row, 8 : 8 + span] = gather(i, row, 8, span)
-
-        loop(XO - DEPTH + i, XO + rows + DEPTH - i, step)
+            grad[i][row, 8 : 8 + span] = gather(i, row, 8, span)
+
+        halves((XO - DEPTH + i, XO + rows + DEPTH - i, step))
 
     def last_step(row):
         final[row] = gather(0, row, YW - 8, cols + 16)
 
-    loop(XO - DEPTH, XO + rows + DEPTH, last_step)
+    halves((XO - DEPTH, XO + rows + DEPTH, last_step))
 
     returns = []
     for k, (dx, dy) in enumerate(DIRS):
@@ -473,7 +496,7 @@
         pl.when(there(dx, dy))(copy.start)
 
     def finish(row):
-        out[row] = final[XO + row, YE : YE + cols] + coef_target * skel[1, row]
+        out[row] = final[XO + row, YE : YE + cols] + coef_target * skel[ITERS][1, row]
 
     loop(0, rows, finish)
 
@@ -505,11 +528,10 @@
         in_specs=[pl.BlockSpec(memory_space=pl.ANY)] * 3,
         out_specs=(pl.BlockSpec(memory_space=pltpu.VMEM), pl.BlockSpec(memory_space=pltpu.VMEM)),
         scratch_shapes=[
-            pltpu.VMEM((STAGES + 1, 2, wide, cols + 16, planes), f32),
+            [pltpu.VMEM((2, wide, cols + 16, planes), f32)] * (STAGES + 1),
             pltpu.VMEM((rows, cols, planes), jnp.int32),
             pltpu.VMEM((rows, cols, planes), f32),
-            pltpu.VMEM((2, rows, cols, planes), f32),
-            pltpu.VMEM((STAGES, rows, cols, planes), f32),
+            [pltpu.VMEM((2, rows, cols, planes), f32)] * STAGES,
             pltpu.VMEM((STAGES, rows, cols, planes), f32),
             pltpu.VMEM((STAGES, rows, cols, planes), f32),
             pltpu.VMEM((STAGES, rows, cols + 8, planes), f32),
@@ -517,7 +539,8 @@
             pltpu.VMEM((STAGES, 3, wide, cols + 8, planes), f32),
             pltpu.VMEM((STAGES, 3, rows, cols + 24, planes), f32),
             pltpu.VMEM((STAGES, 3, rows, cols, planes), f32),
-            pltpu.VMEM((STAGES + 1, wide, cols + 24, planes), f32),
+            [pltpu.VMEM((wide, cols + 24, planes), f32)] * (STAGES + 1),
+            [pltpu.VMEM((wide, cols + 24, planes), f32)] * STAGES,
             pltpu.VMEM((STAGES, rows, cols + 24, planes), f32),
             pltpu.VMEM((STAGES, wide, cols + 8, planes), f32),
             pltpu.VMEM((wide, cols + 16, planes), f32),

time: 43.2 us -> 33.7 us (0.78); the launches traced: 42.6 us -> 33.5 us
  Pallas kernels: 38.6 us -> 29.5 us
    pallas_call x1, Pallas kernels: 38.6 us -> 29.5 us  [body(): pl.pallas_call(functools.partial(kernel, (rows, cols, planes, ngx, ngy)),...]
where the time goes in v1:
time: 33.7 us; the launch traced here: 33.5 us
  Pallas kernels  29.5 us (88%)
  between operations  2.45 us (7%)
  local copies, waits for them, and re-layouts  1.57 us (5%)
    pallas_call x1, Pallas kernels, body(): pl.pallas_call(functools.partial(kernel, (rows, cols, planes, ngx, ngy)),...  29.5 us
    unnamed x1, local copies, waits for them, and re-layouts  1.57 us

profile of v1, /device:TPU:0, one launch (start us, length us, event | category | flops | bytes accessed | tf_op | source)
XLA Modules:
  0.0 33.5 jit_solution(9073393418691766490)
XLA Ops:
  0.6 29.5 %shard_map.50 = (f32[16,16,128]{2,1,0:T(8,128)}, f32[1,1]{1,0:T(1,128)}) custom-call(f32[16,16,128]{2,1,0:T(8,128)} %pred_hbm.1, s32[16,16,128]{2,1,0:T(8,128)} %label_hbm.1, f32[16,16,128]{2,1,0:T(8,128)} %conf_hbm.1), custom_call_target="tpu_custom_call" | custom-call | tf_op jit(solution)/shard_map/pallas_call | solution.py:525
  30.2 1.6 %copy.7 = f32[16,16,128]{2,1,0:T(8,128)} copy(f32[16,16,128]{2,1,0:T(8,128)} %get-tuple-element.8) | data formatting | bytes 262144

commit v2 on v1

--- a/solution.py
+++ b/solution.py
@@ -56,7 +56,7 @@
 def kernel(
     sizes, pred_hbm, label_hbm, conf_hbm, out, loss,
     vol, lab, conf, skel, dels, coefs, pool, wgt, wx, wy, wz, base, grad, hz, hy, final,
-    part, slots_y, slots_x, got_x, got_y, got_c,
+    part, slots_y, slots_x, got_x, got_y, got_c, edge_out, edge_in, back_out,
     in_sem, halo_send, halo_recv, sy_send, sy_recv, sx_send, sx_recv, g_send, g_recv,
 ):
     rows, cols, planes, ngx, ngy = sizes
@@ -92,14 +92,6 @@
         def _(dx=dx, dy=dy):
             pl.semaphore_signal(barrier, inc=1, device_id=(gx + dx, gy + dy), device_id_type=MESH)
 
-    for copy in loads:
-        copy.wait()
-
-    def make_target(row):
-        vol[0][1, XO + row, YE : YE + cols] = lab[row].astype(jnp.float32) * conf[row]
-
-    loop(0, rows, make_target)
-
     corners = 1
     for me, size in ((gx, ngx), (gy, ngy)):
         corners *= lax.div(me + size - 1, size) + lax.div(2 * size - 2 - me, size)
@@ -112,18 +104,61 @@
             return pl.ds(offset - width if outside else offset, width)
         return pl.ds(offset + length if outside else offset + length - width, width)
 
-    halos = []
-    for k, (dx, dy) in enumerate(DIRS):
-        copy = pltpu.make_async_remote_copy(
-            src_ref=vol[0].at[:, strip(dx, rows, XO, DEPTH, False), strip(dy, cols, YE, 8, False)],
-            dst_ref=vol[0].at[:, strip(-dx, rows, XO, DEPTH, True), strip(-dy, cols, YE, 8, True)],
-            send_sem=halo_send.at[k],
-            recv_sem=halo_recv.at[k],
-            device_id=(gx + dx, gy + dy),
-            device_id_type=MESH,
-        )
-        halos.append(copy)
-        pl.when(there(dx, dy))(copy.start)
+    def corner_strips(dx, dy, outside, x_at, y_at):
+        offset, found = 0, []
+        for i in range(1, DEPTH + 1):
+            width = DEPTH + 1 - i
+            if outside:
+                row = x_at - i if dx < 0 else x_at + rows + i - 1
+                column = y_at - width if dy < 0 else y_at + cols
+            else:
+                row = x_at + i - 1 if dx < 0 else x_at + rows - i
+                column = y_at if dy < 0 else y_at + cols - width
+            found.append((offset, width, row, slice(column, column + width)))
+            offset += width
+        return found
+
+    def send_halo(v):
+        copies = []
+        for k, (dx, dy) in enumerate(DIRS):
+            if dx and dy:
+                for offset, width, row, columns in corner_strips(dx, dy, False, XO, YE):
+                    edge_out[v, k - 4, offset : offset + width] = vol[0][v, row, columns]
+                source, target = edge_out.at[v, k - 4], edge_in.at[v, k - 4]
+            else:
+                source = vol[0].at[v, strip(dx, rows, XO, DEPTH, False), strip(dy, cols, YE, 8, False)]
+                target = vol[0].at[v, strip(-dx, rows, XO, DEPTH, True), strip(-dy, cols, YE, 8, True)]
+            copy = pltpu.make_async_remote_copy(
+                src_ref=source,
+                dst_ref=target,
+                send_sem=halo_send.at[8 * v + k],
+                recv_sem=halo_recv.at[8 * v + k],
+                device_id=(gx + dx, gy + dy),
+                device_id_type=MESH,
+            )
+            copies.append(copy)
+            pl.when(there(dx, dy))(copy.start)
+        return copies
+
+    def wait_halo(v):
+        for k, (dx, dy) in enumerate(DIRS):
+            @pl.when(there(-dx, -dy))
+            def _(k=k, dx=dx, dy=dy):
+                halos[v][k].wait_recv()
+                if dx and dy:
+                    for offset, width, row, columns in corner_strips(-dx, -dy, True, XO, YE):
+                        vol[0][v, row, columns] = edge_in[v, k - 4, offset : offset + width]
+
+    loads[0].wait()
+    halos = [send_halo(0)]
+    loads[1].wait()
+    loads[2].wait()
+
+    def make_target(row):
+        vol[0][1, XO + row, YE : YE + cols] = lab[row].astype(jnp.float32) * conf[row]
+
+    loop(0, rows, make_target, 8)
+    halos.append(send_halo(1))
 
     def clear_grad(row):
         for i in range(STAGES + 1):
@@ -164,28 +199,25 @@
 
     loop(0, rows, clear_pools)
 
-    for k, (dx, dy) in enumerate(DIRS):
-        pl.when(there(-dx, -dy))(halos[k].wait_recv)
-
-    def stand_in(i):
+    def stand_in(i, v):
         reach = DEPTH - i
         every = pl.ds(XO - reach, rows + 2 * reach)
 
         @pl.when(gy == 0)
         def _():
-            vol[i][:, every, YE - 1 : YE] = vol[i][:, every, YE : YE + 1]
+            vol[i][v, every, YE - 1 : YE] = vol[i][v, every, YE : YE + 1]
 
         @pl.when(gy == ngy - 1)
         def _():
-            vol[i][:, every, YE + cols : YE + cols + 1] = vol[i][:, every, YE + cols - 1 : YE + cols]
+            vol[i][v, every, YE + cols : YE + cols + 1] = vol[i][v, every, YE + cols - 1 : YE + cols]
 
         @pl.when(gx == 0)
         def _():
-            vol[i][:, XO - 1] = vol[i][:, XO]
+            vol[i][v, XO - 1] = vol[i][v, XO]
 
         @pl.when(gx == ngx - 1)
         def _():
-            vol[i][:, XO + rows] = vol[i][:, XO + rows - 1]
+            vol[i][v, XO + rows] = vol[i][v, XO + rows - 1]
 
     def before(value, edge):
         return jnp.where(at_first, edge, pltpu.roll(value, 1, 1))
@@ -193,75 +225,49 @@
     def after(value):
         return jnp.where(at_last, value, pltpu.roll(value, planes - 1, 1))
 
-    def erode_step(i):
+    def erode_step(i, v):
         reach = STAGES - i
 
         def step(row):
-            for v in range(2):
-                mid = vol[i][v, row, 4 : 4 + span]
-                least = jnp.minimum(vol[i][v, row - 1, 4 : 4 + span], vol[i][v, row + 1, 4 : 4 + span])
-                sides = jnp.minimum(vol[i][v, row, 3 : 3 + span], vol[i][v, row, 5 : 5 + span])
-                along = jnp.minimum(before(mid, mid), after(mid))
-                vol[i + 1][v, row, 4 : 4 + span] = jnp.minimum(jnp.minimum(least, sides), jnp.minimum(along, mid))
+            mid = vol[i][v, row, 4 : 4 + span]
+            least = jnp.minimum(vol[i][v, row - 1, 4 : 4 + span], vol[i][v, row + 1, 4 : 4 + span])
+            sides = jnp.minimum(vol[i][v, row, 3 : 3 + span], vol[i][v, row, 5 : 5 + span])
+            along = jnp.minimum(before(mid, mid), after(mid))
+            vol[i + 1][v, row, 4 : 4 + span] = jnp.minimum(jnp.minimum(least, sides), jnp.minimum(along, mid))
 
         return XO - reach, XO + rows + reach, step
 
-    def delta_step(i):
+    def delta_step(i, v):
         def step(row):
-            for v in range(2):
-                most = None
-                for x in (-1, 0, 1):
-                    for y in (-1, 0, 1):
-                        value = vol[i + 1][v, XO + row + x, YE + y : YE + y + cols]
-                        most = value if most is None else jnp.maximum(most, value)
-                most = jnp.maximum(jnp.maximum(before(most, most), most), after(most))
-                delta = jnp.maximum(vol[i][v, XO + row, YE : YE + cols] - most, 0.0)
-                if i == 0:
-                    result = delta
-                else:
-                    old = skel[i - 1][v, row]
-                    result = old + jnp.maximum(delta - old * delta, 0.0)
-                skel[i][v, row] = result
-                if v == 0:
-                    dels[i, row] = delta
+            most = None
+            for x in (-1, 0, 1):
+                for y in (-1, 0, 1):
+                    value = vol[i + 1][v, XO + row + x, YE + y : YE + y + cols]
+                    most = value if most is None else jnp.maximum(most, value)
+            most = jnp.maximum(jnp.maximum(before(most, most), most), after(most))
+            delta = jnp.maximum(vol[i][v, XO + row, YE : YE + cols] - most, 0.0)
+            if i == 0:
+                result = delta
+            else:
+                old = skel[i - 1][v, row]
+                result = old + jnp.maximum(delta - old * delta, 0.0)
+            skel[i][v, row] = result
+            if v == 0:
+                dels[i, row] = delta
 
         return 0, rows, step
 
-    stand_in(0)
-    halves(erode_step(0))
-    stand_in(1)
-    for i in range(1, STAGES):
-        halves(delta_step(i - 1), erode_step(i))
-        stand_in(i + 1)
-    halves(delta_step(STAGES - 1))
-
-    def add_up(row, sums):
-        sum_a, sum_b, sum_c, sum_d = sums
-        skel_pred, skel_target = skel[ITERS][0, row], skel[ITERS][1, row]
-        return (
-            sum_a + skel_pred * vol[0][1, XO + row, YE : YE + cols],
-            sum_b + skel_pred,
-            sum_c + skel_target * vol[0][0, XO + row, YE : YE + cols],
-            sum_d + skel_target,
-        )
-
-    sums = (jnp.zeros((cols, planes), jnp.float32),) * 4
-    for row in range(rows):
-        sums = add_up(row, sums)
-    part[...] = jnp.zeros_like(part)
-    for k in range(4):
-        part[k : k + 1] = jnp.sum(sums[k], axis=0, keepdims=True)
-
-    slots_y[gy] = part[...]
-    copies_y = []
-    for k in range(1, ngy):
-        copy = pltpu.make_async_remote_copy(
-            src_ref=part, dst_ref=slots_y.at[gy], send_sem=sy_send.at[k], recv_sem=sy_recv.at[k],
-            device_id=(gx, lax.rem(gy + k, ngy)), device_id_type=MESH,
-        )
-        copy.start()
-        copies_y.append(copy)
-
+    def forward(v):
+        wait_halo(v)
+        stand_in(0, v)
+        halves(erode_step(0, v))
+        stand_in(1, v)
+        for i in range(1, STAGES):
+            halves(delta_step(i - 1, v), erode_step(i, v))
+            stand_in(i + 1, v)
+        halves(delta_step(STAGES - 1, v))
+
+    forward(0)
     def split(total, low, mid, high, first, sign):
         to_high = share(high, first) if sign > 0 else share(first, high)
         to_low = share(low, mid) if sign > 0 else share(mid, low)
@@ -336,6 +342,35 @@
             wx[i, MID, edge] = wx[i, MID, edge] + wx[i, UP, edge]
             wx[i, UP, edge] = jnp.zeros((span, planes), jnp.float32)
 
+    forward(1)
+
+    def add_up(row, sums):
+        sum_a, sum_b, sum_c, sum_d = sums
+        skel_pred, skel_target = skel[ITERS][0, row], skel[ITERS][1, row]
+        return (
+            sum_a + skel_pred * vol[0][1, XO + row, YE : YE + cols],
+            sum_b + skel_pred,
+            sum_c + skel_target * vol[0][0, XO + row, YE : YE + cols],
+            sum_d + skel_target,
+        )
+
+    sums = (jnp.zeros((cols, planes), jnp.float32),) * 4
+    for row in range(rows):
+        sums = add_up(row, sums)
+    part[...] = jnp.zeros_like(part)
+    for k in range(4):
+        part[k : k + 1] = jnp.sum(sums[k], axis=0, keepdims=True)
+
+    slots_y[gy] = part[...]
+    copies_y = []
+    for k in range(1, ngy):
+        copy = pltpu.make_async_remote_copy(
+            src_ref=part, dst_ref=slots_y.at[gy], send_sem=sy_send.at[k], recv_sem=sy_recv.at[k],
+            device_id=(gx, lax.rem(gy + k, ngy)), device_id_type=MESH,
+        )
+        copy.start()
+        copies_y.append(copy)
+
     def erode_weights(i):
         reach = STAGES - i
         every = pl.ds(XO - reach, rows + 2 * reach)
@@ -474,46 +509,60 @@
     def last_step(row):
         final[row] = gather(0, row, YW - 8, cols + 16)
 
-    halves((XO - DEPTH, XO + rows + DEPTH, last_step))
-
-    returns = []
-    for k, (dx, dy) in enumerate(DIRS):
+    def send_back(k):
+        dx, dy = DIRS[k]
         if dx and dy:
-            place = got_c.at[k - 4]
-        elif dx:
-            place = got_x.at[k]
+            for offset, width, row, columns in corner_strips(dx, dy, True, XO, YE):
+                back_out[k - 4, offset : offset + width] = final[row, columns]
+            source, place = back_out.at[k - 4], got_c.at[k - 4]
         else:
-            place = got_y.at[k - 2]
+            source = final.at[strip(dx, rows, XO, DEPTH, True), strip(dy, cols, YE, 8, True)]
+            place = got_x.at[k] if dx else got_y.at[k - 2]
         copy = pltpu.make_async_remote_copy(
-            src_ref=final.at[strip(dx, rows, XO, DEPTH, True), strip(dy, cols, YE, 8, True)],
+            src_ref=source,
             dst_ref=place,
             send_sem=g_send.at[k],
             recv_sem=g_recv.at[k],
             device_id=(gx + dx, gy + dy),
             device_id_type=MESH,
         )
-        returns.append((copy, place))
         pl.when(there(dx, dy))(copy.start)
-
-    def finish(row):
-        out[row] = final[XO + row, YE : YE + cols] + coef_target * skel[ITERS][1, row]
-
-    loop(0, rows, finish)
+        return copy
+
+    returns = {}
+    for side, low in enumerate((XO - DEPTH, XO + rows)):
+        for row in range(low, low + DEPTH):
+            last_step(row)
+        returns[side] = send_back(side)
+    for k in range(4, 8):
+        returns[k] = send_back(k)
+
+    def middle_step(row):
+        value = gather(0, XO + row, YW - 8, cols + 16)
+        final[XO + row] = value
+        out[row] = value[8 : 8 + cols] + coef_target * skel[ITERS][1, row]
+
+    halves((0, rows, middle_step))
+    for k in (2, 3):
+        returns[k] = send_back(k)
 
     for k, (dx, dy) in enumerate(DIRS):
-        copy, place = returns[k]
-
         @pl.when(there(-dx, -dy))
-        def _(copy=copy, place=place, dx=dx, dy=dy):
-            copy.wait_recv()
-            at = (strip(-dx, rows, 0, DEPTH, False), strip(-dy, cols, 0, 8, False))
-            out[at] = out[at] + place[...]
+        def _(k=k, dx=dx, dy=dy):
+            returns[k].wait_recv()
+            if dx and dy:
+                for offset, width, row, columns in corner_strips(-dx, -dy, False, 0, 0):
+                    out[row, columns] = out[row, columns] + got_c[k - 4, offset : offset + width]
+            else:
+                at = (strip(-dx, rows, 0, DEPTH, False), strip(-dy, cols, 0, 8, False))
+                out[at] = out[at] + (got_x[k] if dx else got_y[k - 2])
 
     for k, (dx, dy) in enumerate(DIRS):
         @pl.when(there(dx, dy))
         def _(k=k):
-            halos[k].wait_send()
-            returns[k][0].wait_send()
+            halos[0][k].wait_send()
+            halos[1][k].wait_send()
+            returns[k].wait_send()
 
 
 def body(prediction, label_mask, confidence):
@@ -521,6 +570,7 @@
     ngx, ngy = lax.axis_size("gx"), lax.axis_size("gy")
     f32 = jnp.float32
     wide = rows + 2 * XO
+    corner = (DEPTH * (DEPTH + 1) // 2 + 7) // 8 * 8
     dma = pltpu.SemaphoreType.DMA
     gradient, loss = pl.pallas_call(
         functools.partial(kernel, (rows, cols, planes, ngx, ngy)),
@@ -549,10 +599,13 @@
             pltpu.VMEM((ngx, 8, planes), f32),
             pltpu.VMEM((2, DEPTH, cols, planes), f32),
             pltpu.VMEM((2, rows, 8, planes), f32),
-            pltpu.VMEM((4, DEPTH, 8, planes), f32),
+            pltpu.VMEM((4, corner, planes), f32),
+            pltpu.VMEM((2, 4, corner, planes), f32),
+            pltpu.VMEM((2, 4, corner, planes), f32),
+            pltpu.VMEM((4, corner, planes), f32),
             dma((3,)),
-            dma((8,)),
-            dma((8,)),
+            dma((16,)),
+            dma((16,)),
             dma((ngy,)),
             dma((ngy,)),
             dma((ngx,)),

time: 33.7 us -> 33.1 us (0.982)
  Pallas kernels: 29.5 us -> 28.9 us
    pallas_call x1, Pallas kernels: 29.5 us -> 28.9 us  [body(): pl.pallas_call(functools.partial(kernel, (rows, cols, planes, ngx, ngy)),...]
where the time goes in v2:
time: 33.1 us; the launch traced here: 32.9 us
  Pallas kernels  28.9 us (87%)
  between operations  2.45 us (7%)
  local copies, waits for them, and re-layouts  1.57 us (5%)
    pallas_call x1, Pallas kernels, body(): pl.pallas_call(functools.partial(kernel, (rows, cols, planes, ngx, ngy)),...  28.9 us
    unnamed x1, local copies, waits for them, and re-layouts  1.57 us

profile of v2, /device:TPU:0, one launch (start us, length us, event | category | flops | bytes accessed | tf_op | source)
XLA Modules:
  0.0 32.9 jit_solution(12092152304284305341)
XLA Ops:
  0.6 28.9 %shard_map.50 = (f32[16,16,128]{2,1,0:T(8,128)}, f32[1,1]{1,0:T(1,128)}) custom-call(f32[16,16,128]{2,1,0:T(8,128)} %pred_hbm.1, s32[16,16,128]{2,1,0:T(8,128)} %label_hbm.1, f32[16,16,128]{2,1,0:T(8,128)} %conf_hbm.1), custom_call_target="tpu_custom_call" | custom-call | tf_op jit(solution)/shard_map/pallas_call | solution.py:575
  29.6 1.6 %copy.7 = f32[16,16,128]{2,1,0:T(8,128)} copy(f32[16,16,128]{2,1,0:T(8,128)} %get-tuple-element.8) | data formatting | bytes 262144

commit v3 on v2

--- a/solution.py
+++ b/solution.py
@@ -51,6 +51,12 @@
     for low, high, body in parts:
         if (high - low) % 2:
             body(high - 1)
+
+
+def straight(*parts):
+    for low, high, body in parts:
+        for row in range(low, high):
+            body(row)
 
 
 def kernel(
@@ -227,13 +233,26 @@
 
     def erode_step(i, v):
         reach = STAGES - i
-
-        def step(row):
+        done = vol[i + 1]
+
+        def eroded(row):
             mid = vol[i][v, row, 4 : 4 + span]
             least = jnp.minimum(vol[i][v, row - 1, 4 : 4 + span], vol[i][v, row + 1, 4 : 4 + span])
             sides = jnp.minimum(vol[i][v, row, 3 : 3 + span], vol[i][v, row, 5 : 5 + span])
             along = jnp.minimum(before(mid, mid), after(mid))
-            vol[i + 1][v, row, 4 : 4 + span] = jnp.minimum(jnp.minimum(least, sides), jnp.minimum(along, mid))
+            return jnp.minimum(jnp.minimum(least, sides), jnp.minimum(along, mid))
+
+        def step(row):
+            value = eroded(row)
+            if row == XO - 1:
+                value = jnp.where(gx == 0, eroded(XO), value)
+            if row == XO + rows:
+                value = jnp.where(gx == ngx - 1, eroded(XO + rows - 1), value)
+            done[v, row, 4 : 4 + span] = value
+            for place, inner, found in ((YE - 1, YE, gy == 0), (YE + cols, YE + cols - 1, gy == ngy - 1)):
+                done[v, row, place : place + 1] = jnp.where(
+                    found, done[v, row, inner : inner + 1], done[v, row, place : place + 1]
+                )
 
         return XO - reach, XO + rows + reach, step
 
@@ -260,12 +279,10 @@
     def forward(v):
         wait_halo(v)
         stand_in(0, v)
-        halves(erode_step(0, v))
-        stand_in(1, v)
+        straight(erode_step(0, v))
         for i in range(1, STAGES):
-            halves(delta_step(i - 1, v), erode_step(i, v))
-            stand_in(i + 1, v)
-        halves(delta_step(STAGES - 1, v))
+            straight(erode_step(i, v), delta_step(i - 1, v))
+        straight(delta_step(STAGES - 1, v))
 
     forward(0)
     def split(total, low, mid, high, first, sign):
@@ -286,7 +303,7 @@
             wx[i, MID, XO + row] = to_mid
             pool[i, row] = jnp.maximum(first, high)
 
-    loop(0, rows, dilate_weights, 2)
+    loop(0, rows, dilate_weights, 4)
 
     def dilate_weights_2(row):
         below = 1.0
@@ -313,34 +330,7 @@
             else:
                 coefs[i, row] = jnp.where(delta > 0.0, below, 0.0)
 
-    loop(0, rows, dilate_weights_2, 2)
-
-    @pl.when(gy == 0)
-    def _():
-        edge = pl.ds(YW, 1)
-        for i in range(STAGES):
-            wy[i, MID, :, edge] = wy[i, MID, :, edge] + wy[i, LO, :, edge]
-            wy[i, LO, :, edge] = jnp.zeros((rows, 1, planes), jnp.float32)
-
-    @pl.when(gy == ngy - 1)
-    def _():
-        edge = pl.ds(YW + cols - 1, 1)
-        for i in range(STAGES):
-            wy[i, MID, :, edge] = wy[i, MID, :, edge] + wy[i, UP, :, edge]
-            wy[i, UP, :, edge] = jnp.zeros((rows, 1, planes), jnp.float32)
-
-    @pl.when(gx == 0)
-    def _():
-        for i in range(STAGES):
-            wx[i, MID, XO] = wx[i, MID, XO] + wx[i, LO, XO]
-            wx[i, LO, XO] = jnp.zeros((span, planes), jnp.float32)
-
-    @pl.when(gx == ngx - 1)
-    def _():
-        edge = XO + rows - 1
-        for i in range(STAGES):
-            wx[i, MID, edge] = wx[i, MID, edge] + wx[i, UP, edge]
-            wx[i, UP, edge] = jnp.zeros((span, planes), jnp.float32)
+    loop(0, rows, dilate_weights_2, 4)
 
     forward(1)
 
@@ -373,7 +363,6 @@
 
     def erode_weights(i):
         reach = STAGES - i
-        every = pl.ds(XO - reach, rows + 2 * reach)
         mine = slice(8, 8 + span)
 
         def step(row):
@@ -399,19 +388,32 @@
             centre = x_parts[2] + y_parts[2] + z_parts[2]
             wgt[i, CC, row, mine] = jnp.where(at_last, centre + z_parts[1], centre)
 
-        loop(XO - reach, XO + rows + reach, step)
-
-        for there_is_none, edge, kind in ((gy == 0, YW, YL), (gy == ngy - 1, YW + cols - 1, YU)):
-            @pl.when(there_is_none)
-            def _(edge=pl.ds(edge, 1), kind=kind):
-                wgt[i, CC, every, edge] = wgt[i, CC, every, edge] + wgt[i, kind, every, edge]
-                wgt[i, kind, every, edge] = jnp.zeros((rows + 2 * reach, 1, planes), jnp.float32)
-
-        for there_is_none, edge, kind in ((gx == 0, XO, XL), (gx == ngx - 1, XO + rows - 1, XU)):
-            @pl.when(there_is_none)
-            def _(edge=edge, kind=kind):
+        halves((XO - reach, XO + rows + reach, step))
+
+    def fold():
+        mine = slice(8, 8 + span)
+
+        def columns(edge, kind, pool_kind):
+            at = pl.ds(edge, 1)
+            for i in range(STAGES):
+                reach = STAGES - i
+                every = pl.ds(XO - reach, rows + 2 * reach)
+                wgt[i, CC, every, at] = wgt[i, CC, every, at] + wgt[i, kind, every, at]
+                wgt[i, kind, every, at] = jnp.zeros((rows + 2 * reach, 1, planes), jnp.float32)
+                wy[i, MID, :, at] = wy[i, MID, :, at] + wy[i, pool_kind, :, at]
+                wy[i, pool_kind, :, at] = jnp.zeros((rows, 1, planes), jnp.float32)
+
+        def along_rows(edge, kind, pool_kind):
+            for i in range(STAGES):
                 wgt[i, CC, edge, mine] = wgt[i, CC, edge, mine] + wgt[i, kind, edge, mine]
                 wgt[i, kind, edge, mine] = jnp.zeros((span, planes), jnp.float32)
+                wx[i, MID, edge] = wx[i, MID, edge] + wx[i, pool_kind, edge]
+                wx[i, pool_kind, edge] = jnp.zeros((span, planes), jnp.float32)
+
+        pl.when(gy == 0)(lambda: columns(YW, YL, LO))
+        pl.when(gy == ngy - 1)(lambda: columns(YW + cols - 1, YU, UP))
+        pl.when(gx == 0)(lambda: along_rows(XO, XL, LO))
+        pl.when(gx == ngx - 1)(lambda: along_rows(XO + rows - 1, XU, UP))
 
     erode_weights(0)
 
@@ -433,6 +435,7 @@
 
     for i in range(1, STAGES):
         erode_weights(i)
+    fold()
 
     for copy in copies_x:
         copy.wait()
@@ -482,7 +485,7 @@
                 + wx[i, UP, row - 1] * hy[i, row - 1]
             )
 
-    halves((XO - 1, XO + rows + 1, back_rows))
+    straight((XO - 1, XO + rows + 1, back_rows))
 
     def gather(i, row, low, length):
         source = grad[i + 1] if i + 1 < STAGES else base[i + 1]
@@ -504,7 +507,7 @@
         def step(row, i=i):
             grad[i][row, 8 : 8 + span] = gather(i, row, 8, span)
 
-        halves((XO - DEPTH + i, XO + rows + DEPTH - i, step))
+        straight((XO - DEPTH + i, XO + rows + DEPTH - i, step))
 
     def last_step(row):
         final[row] = gather(0, row, YW - 8, cols + 16)

time: 33.1 us -> 31.2 us (0.943)
  Pallas kernels: 28.9 us -> 27 us
    pallas_call x1, Pallas kernels: 28.9 us -> 27 us  [body(): pl.pallas_call(functools.partial(kernel, (rows, cols, planes, ngx, ngy)),...]
where the time goes in v3:
time: 31.2 us; the launch traced here: 31 us
  Pallas kernels  27 us (87%)
  between operations  2.45 us (8%)
  local copies, waits for them, and re-layouts  1.57 us (5%)
    pallas_call x1, Pallas kernels, body(): pl.pallas_call(functools.partial(kernel, (rows, cols, planes, ngx, ngy)),...  27 us
    unnamed x1, local copies, waits for them, and re-layouts  1.57 us

profile of v3, /device:TPU:0, one launch (start us, length us, event | category | flops | bytes accessed | tf_op | source)
XLA Modules:
  0.0 31.0 jit_solution(12470701289763281579)
XLA Ops:
  0.6 27.0 %shard_map.50 = (f32[16,16,128]{2,1,0:T(8,128)}, f32[1,1]{1,0:T(1,128)}) custom-call(f32[16,16,128]{2,1,0:T(8,128)} %pred_hbm.1, s32[16,16,128]{2,1,0:T(8,128)} %label_hbm.1, f32[16,16,128]{2,1,0:T(8,128)} %conf_hbm.1), custom_call_target="tpu_custom_call" | custom-call | tf_op jit(solution)/shard_map/pallas_call | solution.py:578
  27.6 1.6 %copy.7 = f32[16,16,128]{2,1,0:T(8,128)} copy(f32[16,16,128]{2,1,0:T(8,128)} %get-tuple-element.8) | data formatting | bytes 262144

commit v4 on v3

--- a/solution.py
+++ b/solution.py
@@ -285,6 +285,35 @@
         straight(delta_step(STAGES - 1, v))
 
     forward(0)
+    forward(1)
+
+    def add_up(row, sums):
+        sum_a, sum_b, sum_c, sum_d = sums
+        skel_pred, skel_target = skel[ITERS][0, row], skel[ITERS][1, row]
+        return (
+            sum_a + skel_pred * vol[0][1, XO + row, YE : YE + cols],
+            sum_b + skel_pred,
+            sum_c + skel_target * vol[0][0, XO + row, YE : YE + cols],
+            sum_d + skel_target,
+        )
+
+    sums = (jnp.zeros((cols, planes), jnp.float32),) * 4
+    for row in range(rows):
+        sums = add_up(row, sums)
+    part[...] = jnp.zeros_like(part)
+    for k in range(4):
+        part[k : k + 1] = jnp.sum(sums[k], axis=0, keepdims=True)
+
+    slots_y[gy] = part[...]
+    copies_y = []
+    for k in range(1, ngy):
+        copy = pltpu.make_async_remote_copy(
+            src_ref=part, dst_ref=slots_y.at[gy], send_sem=sy_send.at[k], recv_sem=sy_recv.at[k],
+            device_id=(gx, lax.rem(gy + k, ngy)), device_id_type=MESH,
+        )
+        copy.start()
+        copies_y.append(copy)
+
     def split(total, low, mid, high, first, sign):
         to_high = share(high, first) if sign > 0 else share(first, high)
         to_low = share(low, mid) if sign > 0 else share(mid, low)
@@ -332,35 +361,6 @@
 
     loop(0, rows, dilate_weights_2, 4)
 
-    forward(1)
-
-    def add_up(row, sums):
-        sum_a, sum_b, sum_c, sum_d = sums
-        skel_pred, skel_target = skel[ITERS][0, row], skel[ITERS][1, row]
-        return (
-            sum_a + skel_pred * vol[0][1, XO + row, YE : YE + cols],
-            sum_b + skel_pred,
-            sum_c + skel_target * vol[0][0, XO + row, YE : YE + cols],
-            sum_d + skel_target,
-        )
-
-    sums = (jnp.zeros((cols, planes), jnp.float32),) * 4
-    for row in range(rows):
-        sums = add_up(row, sums)
-    part[...] = jnp.zeros_like(part)
-    for k in range(4):
-        part[k : k + 1] = jnp.sum(sums[k], axis=0, keepdims=True)
-
-    slots_y[gy] = part[...]
-    copies_y = []
-    for k in range(1, ngy):
-        copy = pltpu.make_async_remote_copy(
-            src_ref=part, dst_ref=slots_y.at[gy], send_sem=sy_send.at[k], recv_sem=sy_recv.at[k],
-            device_id=(gx, lax.rem(gy + k, ngy)), device_id_type=MESH,
-        )
-        copy.start()
-        copies_y.append(copy)
-
     def erode_weights(i):
         reach = STAGES - i
         mine = slice(8, 8 + span)
@@ -578,7 +578,7 @@
     gradient, loss = pl.pallas_call(
         functools.partial(kernel, (rows, cols, planes, ngx, ngy)),
         out_shape=(jax.ShapeDtypeStruct((rows, cols, planes), f32), jax.ShapeDtypeStruct((1, 1), f32)),
-        in_specs=[pl.BlockSpec(memory_space=pl.ANY)] * 3,
+        in_specs=[pl.BlockSpec(memory_space=pltpu.HBM)] * 3,
         out_specs=(pl.BlockSpec(memory_space=pltpu.VMEM), pl.BlockSpec(memory_space=pltpu.VMEM)),
         scratch_shapes=[
             [pltpu.VMEM((2, wide, cols + 16, planes), f32)] * (STAGES + 1),
@@ -617,9 +617,9 @@
             dma((8,)),
         ],
         compiler_params=pltpu.CompilerParams(
-            collective_id=0, has_side_effects=True, vmem_limit_bytes=60 * 1024 * 1024
+            collective_id=0, has_side_effects=True, vmem_limit_bytes=50 * 1024 * 1024
         ),
-    )(prediction, label_mask, confidence)
+    )(*(pltpu.with_memory_space_constraint(value, pltpu.HBM) for value in (prediction, label_mask, confidence)))
     return gradient, loss[0, 0]
 
 

time: 31.2 us -> 29 us (0.929)
  Pallas kernels: 27 us -> 25.8 us
  local copies, waits for them, and re-layouts: 1.57 us -> 0.66 us
    pallas_call x1, Pallas kernels: 27 us -> 25.8 us  [body(): pl.pallas_call(functools.partial(kernel, (rows, cols, planes, ngx, ngy)),...]
    unnamed x1, local copies, waits for them, and re-layouts: 1.57 us -> 0.66 us
where the time goes in v4:
time: 29 us; the launch traced here: 28.8 us
  Pallas kernels  25.8 us (89%)
  between operations  2.33 us (8%)
  local copies, waits for them, and re-layouts  0.66 us (2%)
    pallas_call x1, Pallas kernels, body(): pl.pallas_call(functools.partial(kernel, (rows, cols, planes, ngx, ngy)),...  25.8 us
    unnamed x1, local copies, waits for them, and re-layouts  0.66 us

profile of v4, /device:TPU:0, one launch (start us, length us, event | category | flops | bytes accessed | tf_op | source)
XLA Modules:
  0.0 28.8 jit_solution(8169026347342037662)
XLA Ops:
  0.6 25.8 %shard_map.50 = (f32[16,16,128]{2,1,0:T(8,128)S(1)}, f32[1,1]{1,0:T(1,128)}) custom-call(f32[16,16,128]{2,1,0:T(8,128)} %pred_hbm.1, s32[16,16,128]{2,1,0:T(8,128)} %label_hbm.1, f32[16,16,128]{2,1,0:T(8,128)} %conf_hbm.1), custom_call_target="tpu_custom_call" | custom-call | tf_op jit(solution)/shard_map/pallas_call | solution.py:578
  26.5 0.7 %copy.7 = f32[16,16,128]{2,1,0:T(8,128)} copy(f32[16,16,128]{2,1,0:T(8,128)S(1)} %get-tuple-element.8) | data formatting | bytes 262144

commit v5 on v4

--- a/solution.py
+++ b/solution.py
@@ -234,10 +234,16 @@
     def erode_step(i, v):
         reach = STAGES - i
         done = vol[i + 1]
+        held = {}
+
+        def at(row):
+            if row not in held:
+                held[row] = vol[i][v, row, 4 : 4 + span]
+            return held[row]
 
         def eroded(row):
-            mid = vol[i][v, row, 4 : 4 + span]
-            least = jnp.minimum(vol[i][v, row - 1, 4 : 4 + span], vol[i][v, row + 1, 4 : 4 + span])
+            mid = at(row)
+            least = jnp.minimum(at(row - 1), at(row + 1))
             sides = jnp.minimum(vol[i][v, row, 3 : 3 + span], vol[i][v, row, 5 : 5 + span])
             along = jnp.minimum(before(mid, mid), after(mid))
             return jnp.minimum(jnp.minimum(least, sides), jnp.minimum(along, mid))
@@ -257,12 +263,17 @@
         return XO - reach, XO + rows + reach, step
 
     def delta_step(i, v):
+        held = {}
+
+        def across(row):
+            if row not in held:
+                low, mid, high = [vol[i + 1][v, row, YE + y : YE + y + cols] for y in (-1, 0, 1)]
+                held[row] = jnp.maximum(jnp.maximum(low, mid), high)
+            return held[row]
+
         def step(row):
-            most = None
-            for x in (-1, 0, 1):
-                for y in (-1, 0, 1):
-                    value = vol[i + 1][v, XO + row + x, YE + y : YE + y + cols]
-                    most = value if most is None else jnp.maximum(most, value)
+            row_at = XO + row
+            most = jnp.maximum(jnp.maximum(across(row_at - 1), across(row_at)), across(row_at + 1))
             most = jnp.maximum(jnp.maximum(before(most, most), most), after(most))
             delta = jnp.maximum(vol[i][v, XO + row, YE : YE + cols] - most, 0.0)
             if i == 0:
@@ -465,7 +476,7 @@
                 + pltpu.roll(given * wz[i, UP, row], 1, 1)
             )
 
-    loop(0, rows, start_back, 4)
+    straight((0, rows, start_back))
 
     def back_columns(row):
         for i in range(STAGES):
@@ -475,7 +486,7 @@
                 + wy[i, UP, row, 7 : 7 + span] * hz[i, row, 7 : 7 + span]
             )
 
-    loop(0, rows, back_columns, 4)
+    straight((0, rows, back_columns))
 
     def back_rows(row):
         for i in range(STAGES):
@@ -487,16 +498,22 @@
 
     straight((XO - 1, XO + rows + 1, back_rows))
 
-    def gather(i, row, low, length):
+    def gather(i, row, low, length, held):
         source = grad[i + 1] if i + 1 < STAGES else base[i + 1]
         here = slice(low, low + length)
         up, down = slice(low + 1, low + 1 + length), slice(low - 1, low - 1 + length)
-        value = source[row, here]
+
+        def at(row):
+            if row not in held:
+                held[row] = source[row, here]
+            return held[row]
+
+        value = at(row)
         return (
             base[i][row, here]
             + wgt[i, CC, row, here] * value
-            + wgt[i, XL, row + 1, here] * source[row + 1, here]
-            + wgt[i, XU, row - 1, here] * source[row - 1, here]
+            + wgt[i, XL, row + 1, here] * at(row + 1)
+            + wgt[i, XU, row - 1, here] * at(row - 1)
             + wgt[i, YL, row, up] * source[row, up]
             + wgt[i, YU, row, down] * source[row, down]
             + pltpu.roll(wgt[i, ZL, row, here] * value, planes - 1, 1)
@@ -504,13 +521,17 @@
         )
 
     for i in reversed(range(1, STAGES)):
-        def step(row, i=i):
-            grad[i][row, 8 : 8 + span] = gather(i, row, 8, span)
+        held = {}
+
+        def step(row, i=i, held=held):
+            grad[i][row, 8 : 8 + span] = gather(i, row, 8, span, held)
 
         straight((XO - DEPTH + i, XO + rows + DEPTH - i, step))
 
+    held_sides = {}
+
     def last_step(row):
-        final[row] = gather(0, row, YW - 8, cols + 16)
+        final[row] = gather(0, row, YW - 8, cols + 16, held_sides)
 
     def send_back(k):
         dx, dy = DIRS[k]
@@ -540,14 +561,19 @@
     for k in range(4, 8):
         returns[k] = send_back(k)
 
+    held_low, held_high, held_own = {}, {}, {}
+
+    def side_columns(row):
+        final[row, 0:YE] = gather(0, row, YW - YE, YE, held_low)
+        final[row, YE + cols : cols + 16] = gather(0, row, YW + cols, 8, held_high)
+
     def middle_step(row):
-        value = gather(0, XO + row, YW - 8, cols + 16)
-        final[XO + row] = value
-        out[row] = value[8 : 8 + cols] + coef_target * skel[ITERS][1, row]
-
-    halves((0, rows, middle_step))
+        out[row] = gather(0, XO + row, YW, cols, held_own) + coef_target * skel[ITERS][1, row]
+
+    straight((XO, XO + rows, side_columns))
     for k in (2, 3):
         returns[k] = send_back(k)
+    straight((0, rows, middle_step))
 
     for k, (dx, dy) in enumerate(DIRS):
         @pl.when(there(-dx, -dy))

time: 29 us -> 28.6 us (0.986)
  Pallas kernels: 25.8 us -> 25.5 us
    pallas_call x1, Pallas kernels: 25.8 us -> 25.5 us  [body(): pl.pallas_call(functools.partial(kernel, (rows, cols, planes, ngx, ngy)),...]
where the time goes in v5:
time: 28.6 us; the launch traced here: 28.4 us
  Pallas kernels  25.5 us (89%)
  between operations  2.33 us (8%)
  local copies, waits for them, and re-layouts  0.66 us (2%)
    pallas_call x1, Pallas kernels, body(): pl.pallas_call(functools.partial(kernel, (rows, cols, planes, ngx, ngy)),...  25.5 us
    unnamed x1, local copies, waits for them, and re-layouts  0.66 us

profile of v5, /device:TPU:0, one launch (start us, length us, event | category | flops | bytes accessed | tf_op | source)
XLA Modules:
  0.0 28.4 jit_solution(4715856183248782792)
XLA Ops:
  0.6 25.5 %shard_map.50 = (f32[16,16,128]{2,1,0:T(8,128)S(1)}, f32[1,1]{1,0:T(1,128)}) custom-call(f32[16,16,128]{2,1,0:T(8,128)} %pred_hbm.1, s32[16,16,128]{2,1,0:T(8,128)} %label_hbm.1, f32[16,16,128]{2,1,0:T(8,128)} %conf_hbm.1), custom_call_target="tpu_custom_call" | custom-call | tf_op jit(solution)/shard_map/pallas_call | solution.py:604
  26.1 0.7 %copy.7 = f32[16,16,128]{2,1,0:T(8,128)} copy(f32[16,16,128]{2,1,0:T(8,128)S(1)} %get-tuple-element.8) | data formatting | bytes 262144
